TPU v7x, 32 devices: a whole 2x2x4 slice. The times are simulated.
32 devices in a mesh: groups: 2 (over x), blk: 16 (over z, y, core).
Axes of the slice: x: 2, y: 2, z: 4, core: 2. Of those that a mesh axis runs over, the one named last changes fastest.
Arguments:
- trans_east: float32 [1024, 16, 128], P(('groups', 'blk')), parts along dimension 0, may hold values from 2 to 20
- trans_north: float32 [1024, 16, 128], P(('groups', 'blk')), parts along dimension 0, may hold values from 0.05 to 3
- trans_up: float32 [1024, 16, 128], P(('groups', 'blk')), parts along dimension 0, may hold values from 0.05 to 3
- storage: float32 [1024, 16, 128], P(('groups', 'blk')), parts along dimension 0, may hold values from 0.2 to 4
- support_reach: int32 [64, 8, 4], P(('groups', 'blk')), parts along dimension 0, may hold values from 1 to 16, as said below
Outputs:
- basis_out: float32 [64, 8, 48, 16, 128], P(('groups', 'blk')), parts along dimension 0
There are 2 independent parts, one for each index of `groups`. A program takes and returns all parts, laid end to end along the dimension named above; each array names one. Nothing has to cross between parts.
Inputs may be any that keep to these rules, and one draw needn't show every extreme that they name: `support_reach`: at least one coarse block reaches the full 16 cells in all four directions.
All inputs are finite; a program needn't handle non-finite values.
Results may differ from a plain program's by a relative error of at most 0.0003.
Values sent between devices are 32-bit elements; how exact they have to be, the bound alone decides.
No kernel may reach another device: no remote copies, remote signals or barrier semaphores. Data moves between devices by JAX's collectives and lax.ppermute only.
A program may use at most 128 MiB of HBM per device.

v0:
```python
import jax
import jax.numpy as jnp
from jax import lax
from jax.sharding import PartitionSpec as P

BS = 16
CZ = 8
ITERS = 2


relaxation = 2.0 / 3.0


def shifted(value, axis, steps):
    count = lax.axis_size(axis)
    first, last = (max(0, -steps), min(count, count - steps))
    return lax.ppermute(value, axis, [(source, source + steps) for source in range(first, last)])


def extended_2(x, sides, width):
    for axis, dim in sides:
        count, length = (lax.axis_size(axis), x.shape[dim])
        up = [(i, (i + 1) % count) for i in range(count - 1)]
        down = [(j, i) for i, j in up]
        last = lax.slice_in_dim(x, length - width, length, axis=dim)
        first = lax.slice_in_dim(x, 0, width, axis=dim)
        before = lax.ppermute(last, axis, up)
        after = lax.ppermute(first, axis, down)
        x = jnp.concatenate([before, x, after], axis=dim)
    return x


def next_along(field, axis):
    size = field.shape[axis]
    rest = lax.slice_in_dim(field, 1, size, axis=axis)
    zeros = jnp.zeros_like(lax.slice_in_dim(field, 0, 1, axis=axis))
    return jnp.concatenate([rest, zeros], axis=axis)


def prev_along(field, axis):
    size = field.shape[axis]
    rest = lax.slice_in_dim(field, 0, size - 1, axis=axis)
    zeros = jnp.zeros_like(lax.slice_in_dim(field, 0, 1, axis=axis))
    return jnp.concatenate([zeros, rest], axis=axis)


def apply_box(values, face_x, face_y, face_z, diagonal):
    applied = diagonal * values
    applied = (
        applied - face_x * prev_along(values, 1) - next_along(face_x, 0) * next_along(values, 1)
    )
    applied = (
        applied - face_y * prev_along(values, 2) - next_along(face_y, 1) * next_along(values, 2)
    )
    applied = (
        applied - face_z * prev_along(values, 3) - next_along(face_z, 2) * next_along(values, 3)
    )
    return applied


def support_masks(layer, reach_rows, cells_x, blocks_z):
    plane_pos = jnp.arange(3 * BS, dtype=jnp.int32)
    global_x = BS * (layer - 1) + plane_pos
    in_domain = (global_x >= 0) & (global_x < cells_x)
    along_x = (
        in_domain[None, :]
        & (plane_pos[None, :] >= BS - reach_rows[:, 0:1])
        & (plane_pos[None, :] < 2 * BS + reach_rows[:, 1:2])
    )
    depth_pos = jnp.arange(BS * blocks_z, dtype=jnp.int32)
    block_ids = jnp.arange(blocks_z, dtype=jnp.int32)[:, None]
    along_z = (depth_pos[None, :] >= BS * block_ids - reach_rows[:, 2:3]) & (
        depth_pos[None, :] < BS * block_ids + BS + reach_rows[:, 3:4]
    )
    support = along_x[:, :, None, None] & along_z[:, None, None, :]
    own_x = (plane_pos >= BS) & (plane_pos < 2 * BS)
    own_z = depth_pos[None, :] // BS == block_ids
    initial = own_x[None, :, None, None] & own_z[:, None, None, :]
    initial = jnp.broadcast_to(initial, (blocks_z, 3 * BS, BS, BS * blocks_z)).astype(jnp.float32)
    return (support, in_domain, initial)


def on_device(trans_east, trans_north, trans_up, storage, support_reach):
    planes = lax.axis_size("blk")
    device = lax.axis_index("blk")
    local_layers = support_reach.shape[0]
    is_first = device == 0
    face_x = trans_east.at[0].set(jnp.where(is_first, 0.0, trans_east[0]))
    face_y = trans_north.at[:, 0].set(0.0)
    face_z = trans_up.at[:, :, 0].set(0.0)
    beyond = shifted(face_x[0:1], "blk", -1)
    diagonal = storage + face_x + jnp.concatenate([face_x[1:], beyond], axis=0)
    diagonal = diagonal + face_y + next_along(face_y, 1) + face_z + next_along(face_z, 2)
    coeffs = extended_2(jnp.stack([face_x, face_y, face_z, diagonal]), (("blk", 1),), BS)
    cells_x = BS * local_layers * planes
    supports = []
    bases = []
    diags = []
    for local in range(local_layers):
        layer = device * local_layers + local
        support, in_domain, initial = support_masks(layer, support_reach[local], cells_x, CZ)
        supports.append(support)
        bases.append(initial)
        box_d = coeffs[3, local * BS : local * BS + 3 * BS]
        diags.append(jnp.where(in_domain[:, None, None], box_d, 1.0))
    frame = (local_layers + 2) * BS
    for sweep in range(ITERS):
        updates = []
        partial_value = jnp.zeros((frame,) + trans_east.shape[1:], jnp.float32)
        for local in range(local_layers):
            low = local * BS
            applied = apply_box(
                bases[local],
                coeffs[0, low : low + 3 * BS],
                coeffs[1, low : low + 3 * BS],
                coeffs[2, low : low + 3 * BS],
                diags[local],
            )
            update = jnp.where(
                supports[local], bases[local] - relaxation * applied / diags[local], 0.0
            )
            updates.append(update)
            partial_value = partial_value.at[low : low + 3 * BS].add(jnp.sum(update, axis=0))
        extended = extended_2(partial_value, (("blk", 0),), BS)
        own_total = partial_value[BS : frame - BS]
        own_total = own_total.at[0:BS].add(extended[0:BS])
        own_total = own_total.at[-BS:].add(extended[frame + BS : frame + 2 * BS])
        totals = extended_2(own_total, (("blk", 0),), BS)
        for local in range(local_layers):
            low = local * BS
            window = totals[low : low + 3 * BS][None]
            bases[local] = jnp.where(
                supports[local], updates[local] / jnp.where(supports[local], window, 1.0), 0.0
            )
    return jnp.stack(bases)


def solution(mesh):
    in_specs = (
        P(("groups", "blk"), None, None),
        P(("groups", "blk"), None, None),
        P(("groups", "blk"), None, None),
        P(("groups", "blk"), None, None),
        P(("groups", "blk"), None, None),
    )
    out_specs = P(("groups", "blk"), None, None, None, None)
    return jax.shard_map(
        on_device, mesh=mesh, in_specs=in_specs, out_specs=out_specs, check_vma=False
    )
```

profile of v0, /device:TPU:8, one launch (start us, length us, event | category | flops | bytes accessed | tf_op | source)
XLA Modules:
  0.0 110.2 jit_solution(1224335802806963869)
XLA Ops:
  0.0 1.0 copy.16
  1.0 0.9 copy.18
  2.0 2.7 %collective-permute-start = (f32[1,16,128]{2,1,0:T(8,128)S(1)}, f32[1,16,128]{2,1,0:T(8,128)S(1)}, u32[]{:S(2)}, u32[]{:S(2)}) collective-permute-start(f32[1,16,128]{2,1,0:T(8,128)S(1)} %get-tuple-element.150), channel_id=1, source_target_pairs={{1,0},{2,1},{3,2},{4,3},{5,4},{6,5},{7,6},{8,7},{9,8},{10,9},{11,1... | collective-permute-start | bytes 24584 | tf_op jit(solution)/shard_map/ppermute | solution.py:17
  4.8 0.7 slice_bitcast_fusion.9
  6.1 0.2 scatter.14
  7.0 2.1 %collective-permute-start.1 = (f32[4,16,16,128]{3,2,1,0:T(8,128)S(1)}, f32[4,16,16,128]{3,2,1,0:T(8,128)S(1)}, u32[]{:S(2)}, u32[]{:S(2)}) collective-permute-start(f32[4,16,16,128]{3,2,1,0:T(8,128)S(1)} %get-tuple-element.173), channel_id=1, source_target_pairs={{0,1},{1,2},{2,3},{3,4},{4,5},{5,6},{6,7},{7,8},{8,9},{9,10},{10,1... | collective-permute-start | bytes 1572872 | tf_op jit(solution)/shard_map/ppermute | solution.py:27
  9.1 4.3 %collective-permute-start.2 = (f32[4,16,16,128]{3,2,1,0:T(8,128)S(1)}, f32[4,16,16,128]{3,2,1,0:T(8,128)S(1)}, u32[]{:S(2)}, u32[]{:S(2)}) collective-permute-start(f32[4,16,16,128]{3,2,1,0:T(8,128)S(1)} %get-tuple-element.174), channel_id=1, source_target_pairs={{1,0},{2,1},{3,2},{4,3},{5,4},{6,5},{7,6},{8,7},{9,8},{10,9},{11,1... | collective-permute-start | bytes 1572872 | tf_op jit(solution)/shard_map/ppermute | solution.py:28
  13.7 4.7 %collective-permute-done.1 = f32[4,16,16,128]{3,2,1,0:T(8,128)S(1)} collective-permute-done((f32[4,16,16,128]{3,2,1,0:T(8,128)S(1)}, f32[4,16,16,128]{3,2,1,0:T(8,128)S(1)}, u32[]{:S(2)}, u32[]{:S(2)}) %collective-permute-start.1) | collective-permute-done | bytes 524320 | tf_op jit(solution)/shard_map/ppermute | solution.py:27
  18.5 1.7 %collective-permute-done.2 = f32[4,16,16,128]{3,2,1,0:T(8,128)S(1)} collective-permute-done((f32[4,16,16,128]{3,2,1,0:T(8,128)S(1)}, f32[4,16,16,128]{3,2,1,0:T(8,128)S(1)}, u32[]{:S(2)}, u32[]{:S(2)}) %collective-permute-start.2) | collective-permute-done | bytes 524320 | tf_op jit(solution)/shard_map/ppermute | solution.py:28
  20.2 0.3 maximum_maximum_fusion
  20.5 0.3 fusion.22
  21.0 0.2 slice.547
  21.3 0.2 slice.556
  21.6 0.2 broadcast_in_dim.190
  21.8 0.2 broadcast_in_dim.191
  22.0 0.2 broadcast_in_dim.188
  22.2 0.2 broadcast_in_dim.189
  22.4 0.2 slice.488
  22.7 4.1 %fusion.40 = (f32[48,16,128]{2,1,0:T(8,128)}, f32[8,48,16,128]{3,2,1,0:T(8,128)S(1)}) fusion(f32[8,48,16,127]{3,2,1,0:T(8,128)S(1)} %broadcast_in_dim.191, f32[48,16,128]{2,1,0:T(8,128)S(1)} %concatenate.153, f32[8,48,16,127]{3,2,1,0:T(8,128)S(1)} %broadcast_in_dim.190, f32[48,16,128]{2,1,0:T(8,128)S(1)} %get-tuple-element.199, ...), kind=kLoop, calls=%fused_computation.117 | loop fusion | flops 14057472 | bytes 21889024 | tf_op jit(solution)/shard_map/reduce_sum | solution.py:123
  26.8 3.4 %fusion.42 = (f32[48,16,128]{2,1,0:T(8,128)S(1)}, f32[8,48,16,128]{3,2,1,0:T(8,128)S(1)}) fusion(f32[8,48,16,127]{3,2,1,0:T(8,128)S(1)} %broadcast_in_dim.191, f32[48,16,128]{2,1,0:T(8,128)S(1)} %concatenate.158, f32[8,48,16,127]{3,2,1,0:T(8,128)S(1)} %broadcast_in_dim.190, f32[48,16,128]{2,1,0:T(8,128)S(1)} %get-tuple-element.168, ...), kind=kLoop, calls=%fused_computation.118 | loop fusion | flops 14057472 | bytes 21889024 | tf_op jit(solution)/shard_map/reduce_sum | solution.py:123
  30.3 5.5 %collective-permute-start.3 = (f32[16,16,128]{2,1,0:T(8,128)S(1)}, f32[16,16,128]{2,1,0:T(8,128)S(1)}, u32[]{:S(2)}, u32[]{:S(2)}) collective-permute-start(f32[16,16,128]{2,1,0:T(8,128)S(1)} %slice.559), channel_id=1, source_target_pairs={{0,1},{1,2},{2,3},{3,4},{4,5},{5,6},{6,7},{7,8},{8,9},{9,10},{10,1... | collective-permute-start | bytes 393224 | tf_op jit(solution)/shard_map/ppermute | solution.py:27
  35.9 1.9 %collective-permute-start.4 = (f32[16,16,128]{2,1,0:T(8,128)S(1)}, f32[16,16,128]{2,1,0:T(8,128)S(1)}, u32[]{:S(2)}, u32[]{:S(2)}) collective-permute-start(f32[16,16,128]{2,1,0:T(8,128)S(1)} %slice.561), channel_id=1, source_target_pairs={{1,0},{2,1},{3,2},{4,3},{5,4},{6,5},{7,6},{8,7},{9,8},{10,9},{11,1... | collective-permute-start | bytes 393224 | tf_op jit(solution)/shard_map/ppermute | solution.py:28
  37.8 2.5 %collective-permute-done.4 = f32[16,16,128]{2,1,0:T(8,128)S(1)} collective-permute-done((f32[16,16,128]{2,1,0:T(8,128)S(1)}, f32[16,16,128]{2,1,0:T(8,128)S(1)}, u32[]{:S(2)}, u32[]{:S(2)}) %collective-permute-start.4) | collective-permute-done | bytes 131104 | tf_op jit(solution)/shard_map/ppermute | solution.py:28
  40.4 4.7 %collective-permute-start.6 = (f32[16,16,128]{2,1,0:T(8,128)S(1)}, f32[16,16,128]{2,1,0:T(8,128)S(1)}, u32[]{:S(2)}, u32[]{:S(2)}) collective-permute-start(f32[16,16,128]{2,1,0:T(8,128)S(1)} %slice.568), channel_id=1, source_target_pairs={{1,0},{2,1},{3,2},{4,3},{5,4},{6,5},{7,6},{8,7},{9,8},{10,9},{11,1... | collective-permute-start | bytes 393224 | tf_op jit(solution)/shard_map/ppermute | solution.py:28
  45.1 2.1 %collective-permute-start.5 = (f32[16,16,128]{2,1,0:T(8,128)S(1)}, f32[16,16,128]{2,1,0:T(8,128)S(1)}, u32[]{:S(2)}, u32[]{:S(2)}) collective-permute-start(f32[16,16,128]{2,1,0:T(8,128)S(1)} %get-tuple-element.144), channel_id=1, source_target_pairs={{0,1},{1,2},{2,3},{3,4},{4,5},{5,6},{6,7},{7,8},{8,9},{9,10},{10,1... | collective-permute-start | bytes 393224 | tf_op jit(solution)/shard_map/ppermute | solution.py:27
  47.2 0.4 collective-permute-done.6
  47.6 4.7 %collective-permute-done.5 = f32[16,16,128]{2,1,0:T(8,128)S(1)} collective-permute-done((f32[16,16,128]{2,1,0:T(8,128)S(1)}, f32[16,16,128]{2,1,0:T(8,128)S(1)}, u32[]{:S(2)}, u32[]{:S(2)}) %collective-permute-start.5) | collective-permute-done | bytes 131104 | tf_op jit(solution)/shard_map/ppermute | solution.py:27
  52.3 0.7 divide_select_fusion.1
  53.0 3.3 %fusion.45 = (f32[8,48,15,128]{3,2,1,0:T(8,128)}, f32[8,48,15,128]{3,2,1,0:T(8,128)}) fusion(f32[8,48,16,128]{3,2,1,0:T(8,128)S(1)} %divide_select_fusion.1), kind=kLoop, calls=%fused_computation.120 | loop fusion | bytes 11796480 | tf_op jit(solution)/shard_map/slice | solution.py:42
  56.4 3.8 %fusion.46 = (f32[8,48,16,127]{3,2,1,0:T(8,128)}, f32[8,48,16,127]{3,2,1,0:T(8,128)}) fusion(f32[8,48,16,128]{3,2,1,0:T(8,128)S(1)} %divide_select_fusion.1), kind=kLoop, calls=%fused_computation.121 | loop fusion | bytes 12484608 | tf_op jit(solution)/shard_map/slice | solution.py:42
  60.2 3.1 %fusion.44 = (f32[8,47,16,128]{3,2,1,0:T(8,128)}, f32[8,47,16,128]{3,2,1,0:T(8,128)}) fusion(f32[8,48,16,128]{3,2,1,0:T(8,128)S(1)} %divide_select_fusion.1), kind=kLoop, calls=%fused_computation.119 | loop fusion | bytes 12320768 | tf_op jit(solution)/shard_map/slice | solution.py:42
  63.3 0.7 divide_select_fusion
  64.0 0.6 fusion.48
  64.6 1.1 fusion.49
  65.7 3.1 %fusion.47 = (f32[8,47,16,128]{3,2,1,0:T(8,128)}, f32[8,47,16,128]{3,2,1,0:T(8,128)}) fusion(f32[8,48,16,128]{3,2,1,0:T(8,128)S(1)} %divide_select_fusion), kind=kLoop, calls=%fused_computation.122 | loop fusion | bytes 12320768 | tf_op jit(solution)/shard_map/slice | solution.py:42
  68.7 9.7 %fusion.38 = (f32[48,16,128]{2,1,0:T(8,128)}, f32[8,48,16,128]{3,2,1,0:T(8,128)S(1)}) fusion(f32[8,48,16,127]{3,2,1,0:T(8,128)} %get-tuple-element.156, f32[48,16,128]{2,1,0:T(8,128)} %copy-done.7, f32[8,48,16,127]{3,2,1,0:T(8,128)} %get-tuple-element.155, f32[48,16,128]{2,1,0:T(8,128)S(1)} %get-tuple-element.199, ...), kind=kLoop, calls=%fused_computation.115 | loop fusion | flops 16416768 | bytes 28180480 | tf_op jit(solution)/shard_map/reduce_sum | solution.py:123
  78.4 5.9 %fusion.39 = (f32[48,16,128]{2,1,0:T(8,128)S(1)}, f32[8,48,16,128]{3,2,1,0:T(8,128)S(1)}) fusion(f32[8,48,16,127]{3,2,1,0:T(8,128)S(1)} %get-tuple-element.162, f32[48,16,128]{2,1,0:T(8,128)} %copy-done.4, f32[8,48,16,127]{3,2,1,0:T(8,128)S(1)} %get-tuple-element.161, f32[48,16,128]{2,1,0:T(8,128)S(1)} %get-tuple-element.168, ...), kind=kLoop, calls=%fused_computation.116 | loop fusion | flops 16416768 | bytes 28180480 | tf_op jit(solution)/shard_map/reduce_sum | solution.py:123
  84.4 1.9 %collective-permute-start.7 = (f32[16,16,128]{2,1,0:T(8,128)S(1)}, f32[16,16,128]{2,1,0:T(8,128)S(1)}, u32[]{:S(2)}, u32[]{:S(2)}) collective-permute-start(f32[16,16,128]{2,1,0:T(8,128)S(1)} %slice.577), channel_id=1, source_target_pairs={{0,1},{1,2},{2,3},{3,4},{4,5},{5,6},{6,7},{7,8},{8,9},{9,10},{10,1... | collective-permute-start | bytes 393224 | tf_op jit(solution)/shard_map/ppermute | solution.py:27
  86.4 4.5 %collective-permute-start.8 = (f32[16,16,128]{2,1,0:T(8,128)S(1)}, f32[16,16,128]{2,1,0:T(8,128)S(1)}, u32[]{:S(2)}, u32[]{:S(2)}) collective-permute-start(f32[16,16,128]{2,1,0:T(8,128)S(1)} %slice.579), channel_id=1, source_target_pairs={{1,0},{2,1},{3,2},{4,3},{5,4},{6,5},{7,6},{8,7},{9,8},{10,9},{11,1... | collective-permute-start | bytes 393224 | tf_op jit(solution)/shard_map/ppermute | solution.py:28
  90.9 0.7 collective-permute-done.7
  91.6 1.8 %collective-permute-done.8 = f32[16,16,128]{2,1,0:T(8,128)S(1)} collective-permute-done((f32[16,16,128]{2,1,0:T(8,128)S(1)}, f32[16,16,128]{2,1,0:T(8,128)S(1)}, u32[]{:S(2)}, u32[]{:S(2)}) %collective-permute-start.8) | collective-permute-done | bytes 131104 | tf_op jit(solution)/shard_map/ppermute | solution.py:28
  93.5 4.7 %collective-permute-start.10 = (f32[16,16,128]{2,1,0:T(8,128)S(1)}, f32[16,16,128]{2,1,0:T(8,128)S(1)}, u32[]{:S(2)}, u32[]{:S(2)}) collective-permute-start(f32[16,16,128]{2,1,0:T(8,128)S(1)} %slice.580), channel_id=1, source_target_pairs={{1,0},{2,1},{3,2},{4,3},{5,4},{6,5},{7,6},{8,7},{9,8},{10,9},{11,1... | collective-permute-start | bytes 393224 | tf_op jit(solution)/shard_map/ppermute | solution.py:28
  98.2 1.9 %collective-permute-start.9 = (f32[16,16,128]{2,1,0:T(8,128)S(1)}, f32[16,16,128]{2,1,0:T(8,128)S(1)}, u32[]{:S(2)}, u32[]{:S(2)}) collective-permute-start(f32[16,16,128]{2,1,0:T(8,128)S(1)} %get-tuple-element.138), channel_id=1, source_target_pairs={{0,1},{1,2},{2,3},{3,4},{4,5},{5,6},{6,7},{7,8},{8,9},{9,10},{10,1... | collective-permute-start | bytes 393224 | tf_op jit(solution)/shard_map/ppermute | solution.py:27
  100.1 0.6 collective-permute-done.10
  100.7 4.7 %collective-permute-done.9 = f32[16,16,128]{2,1,0:T(8,128)S(1)} collective-permute-done((f32[16,16,128]{2,1,0:T(8,128)S(1)}, f32[16,16,128]{2,1,0:T(8,128)S(1)}, u32[]{:S(2)}, u32[]{:S(2)}) %collective-permute-start.9) | collective-permute-done | bytes 131104 | tf_op jit(solution)/shard_map/ppermute | solution.py:27
  105.4 0.7 select_bitcast_fusion.1
  106.1 0.7 select_bitcast_fusion
  106.9 3.4 %pad_maximum_fusion = f32[2,8,48,16,128]{4,3,2,1,0:T(8,128)} fusion(f32[1,8,48,16,128]{4,3,2,1,0:T(8,128)S(1)} %select_bitcast_fusion, f32[1,8,48,16,128]{4,3,2,1,0:T(8,128)S(1)} %select_bitcast_fusion.1), kind=kLoop, calls=%fused_computation | loop fusion | flops 1572864 | bytes 12582912 | tf_op jit(solution)/shard_map/stack | solution.py:135
  (82 shorter events, 2.2 us)
Async XLA Ops:
  0.0 6.5 %copy-start = (f32[32,16,128]{2,1,0:T(8,128)S(1)}, f32[32,16,128]{2,1,0:T(8,128)}, u32[]{:S(2)}) copy-start(f32[32,16,128]{2,1,0:T(8,128)} %param.28) | copy-start | bytes 786436
  0.0 6.6 %copy-start.14 = (f32[32,16,128]{2,1,0:T(8,128)S(1)}, f32[32,16,128]{2,1,0:T(8,128)}, u32[]{:S(2)}) copy-start(f32[32,16,128]{2,1,0:T(8,128)} %param.30) | copy-start | bytes 786436
  2.0 4.6 %collective-permute-start = (f32[1,16,128]{2,1,0:T(8,128)S(1)}, f32[1,16,128]{2,1,0:T(8,128)S(1)}, u32[]{:S(2)}, u32[]{:S(2)}) collective-permute-start(f32[1,16,128]{2,1,0:T(8,128)S(1)} %get-tuple-element.150), channel_id=1, source_target_pairs={{1,0},{2,1},{3,2},{4,3},{5,4},{6,5},{7,6},{8,7},{9,8},{10,9},{11,1... | collective-permute-start | bytes 24584 | tf_op jit(solution)/shard_map/ppermute | solution.py:17
  7.0 11.5 %collective-permute-start.1 = (f32[4,16,16,128]{3,2,1,0:T(8,128)S(1)}, f32[4,16,16,128]{3,2,1,0:T(8,128)S(1)}, u32[]{:S(2)}, u32[]{:S(2)}) collective-permute-start(f32[4,16,16,128]{3,2,1,0:T(8,128)S(1)} %get-tuple-element.173), channel_id=1, source_target_pairs={{0,1},{1,2},{2,3},{3,4},{4,5},{5,6},{6,7},{7,8},{8,9},{9,10},{10,1... | collective-permute-start | bytes 1572872 | tf_op jit(solution)/shard_map/ppermute | solution.py:27
  9.1 11.1 %collective-permute-start.2 = (f32[4,16,16,128]{3,2,1,0:T(8,128)S(1)}, f32[4,16,16,128]{3,2,1,0:T(8,128)S(1)}, u32[]{:S(2)}, u32[]{:S(2)}) collective-permute-start(f32[4,16,16,128]{3,2,1,0:T(8,128)S(1)} %get-tuple-element.174), channel_id=1, source_target_pairs={{1,0},{2,1},{3,2},{4,3},{5,4},{6,5},{7,6},{8,7},{9,8},{10,9},{11,1... | collective-permute-start | bytes 1572872 | tf_op jit(solution)/shard_map/ppermute | solution.py:28
  20.8 1.8 %copy-start.10 = (f32[48,16,128]{2,1,0:T(8,128)}, f32[48,16,128]{2,1,0:T(8,128)S(1)}, u32[]{:S(2)}) copy-start(f32[48,16,128]{2,1,0:T(8,128)S(1)} %get-tuple-element.197) | copy-start | bytes 1179652
  20.8 1.8 %copy-start.11 = (f32[48,16,128]{2,1,0:T(8,128)}, f32[48,16,128]{2,1,0:T(8,128)S(1)}, u32[]{:S(2)}) copy-start(f32[48,16,128]{2,1,0:T(8,128)S(1)} %get-tuple-element.200) | copy-start | bytes 1179652
  20.9 5.9 %copy-start.8 = (f32[48,16,128]{2,1,0:T(8,128)}, f32[48,16,128]{2,1,0:T(8,128)S(1)}, u32[]{:S(2)}) copy-start(f32[48,16,128]{2,1,0:T(8,128)S(1)} %get-tuple-element.167) | copy-start | bytes 1179652
  20.9 5.9 %copy-start.9 = (f32[48,16,128]{2,1,0:T(8,128)}, f32[48,16,128]{2,1,0:T(8,128)S(1)}, u32[]{:S(2)}) copy-start(f32[48,16,128]{2,1,0:T(8,128)S(1)} %get-tuple-element.170) | copy-start | bytes 1179652
  20.9 1.7 %copy-start.5 = (f32[48,16,128]{2,1,0:T(8,128)}, f32[48,16,128]{2,1,0:T(8,128)S(1)}, u32[]{:S(2)}) copy-start(f32[48,16,128]{2,1,0:T(8,128)S(1)} %concatenate.147) | copy-start | bytes 1179652
  21.0 1.7 %copy-start.6 = (f32[48,16,128]{2,1,0:T(8,128)}, f32[48,16,128]{2,1,0:T(8,128)S(1)}, u32[]{:S(2)}) copy-start(f32[48,16,128]{2,1,0:T(8,128)S(1)} %concatenate.150) | copy-start | bytes 1179652
  21.2 1.5 %copy-start.7 = (f32[48,16,128]{2,1,0:T(8,128)}, f32[48,16,128]{2,1,0:T(8,128)S(1)}, u32[]{:S(2)}) copy-start(f32[48,16,128]{2,1,0:T(8,128)S(1)} %concatenate.153) | copy-start | bytes 1179652
  21.3 5.5 %copy-start.2 = (f32[48,16,128]{2,1,0:T(8,128)}, f32[48,16,128]{2,1,0:T(8,128)S(1)}, u32[]{:S(2)}) copy-start(f32[48,16,128]{2,1,0:T(8,128)S(1)} %concatenate.156) | copy-start | bytes 1179652
  21.3 5.4 %copy-start.3 = (f32[48,16,128]{2,1,0:T(8,128)}, f32[48,16,128]{2,1,0:T(8,128)S(1)}, u32[]{:S(2)}) copy-start(f32[48,16,128]{2,1,0:T(8,128)S(1)} %concatenate.157) | copy-start | bytes 1179652
  21.6 5.2 %copy-start.4 = (f32[48,16,128]{2,1,0:T(8,128)}, f32[48,16,128]{2,1,0:T(8,128)S(1)}, u32[]{:S(2)}) copy-start(f32[48,16,128]{2,1,0:T(8,128)S(1)} %concatenate.158) | copy-start | bytes 1179652
  26.8 3.4 %copy-start.13 = (f32[48,16,128]{2,1,0:T(8,128)S(1)}, f32[48,16,128]{2,1,0:T(8,128)}, u32[]{:S(2)}) copy-start(f32[48,16,128]{2,1,0:T(8,128)} %get-tuple-element.145) | copy-start | bytes 1179652
  30.3 7.5 %collective-permute-start.3 = (f32[16,16,128]{2,1,0:T(8,128)S(1)}, f32[16,16,128]{2,1,0:T(8,128)S(1)}, u32[]{:S(2)}, u32[]{:S(2)}) collective-permute-start(f32[16,16,128]{2,1,0:T(8,128)S(1)} %slice.559), channel_id=1, source_target_pairs={{0,1},{1,2},{2,3},{3,4},{4,5},{5,6},{6,7},{7,8},{8,9},{9,10},{10,1... | collective-permute-start | bytes 393224 | tf_op jit(solution)/shard_map/ppermute | solution.py:27
  35.9 4.4 %collective-permute-start.4 = (f32[16,16,128]{2,1,0:T(8,128)S(1)}, f32[16,16,128]{2,1,0:T(8,128)S(1)}, u32[]{:S(2)}, u32[]{:S(2)}) collective-permute-start(f32[16,16,128]{2,1,0:T(8,128)S(1)} %slice.561), channel_id=1, source_target_pairs={{1,0},{2,1},{3,2},{4,3},{5,4},{6,5},{7,6},{8,7},{9,8},{10,9},{11,1... | collective-permute-start | bytes 393224 | tf_op jit(solution)/shard_map/ppermute | solution.py:28
  40.4 7.2 %collective-permute-start.6 = (f32[16,16,128]{2,1,0:T(8,128)S(1)}, f32[16,16,128]{2,1,0:T(8,128)S(1)}, u32[]{:S(2)}, u32[]{:S(2)}) collective-permute-start(f32[16,16,128]{2,1,0:T(8,128)S(1)} %slice.568), channel_id=1, source_target_pairs={{1,0},{2,1},{3,2},{4,3},{5,4},{6,5},{7,6},{8,7},{9,8},{10,9},{11,1... | collective-permute-start | bytes 393224 | tf_op jit(solution)/shard_map/ppermute | solution.py:28
  45.1 7.2 %collective-permute-start.5 = (f32[16,16,128]{2,1,0:T(8,128)S(1)}, f32[16,16,128]{2,1,0:T(8,128)S(1)}, u32[]{:S(2)}, u32[]{:S(2)}) collective-permute-start(f32[16,16,128]{2,1,0:T(8,128)S(1)} %get-tuple-element.144), channel_id=1, source_target_pairs={{0,1},{1,2},{2,3},{3,4},{4,5},{5,6},{6,7},{7,8},{8,9},{9,10},{10,1... | collective-permute-start | bytes 393224 | tf_op jit(solution)/shard_map/ppermute | solution.py:27
  52.3 0.7 copy-start.1
  78.4 5.9 %copy-start.12 = (f32[48,16,128]{2,1,0:T(8,128)S(1)}, f32[48,16,128]{2,1,0:T(8,128)}, u32[]{:S(2)}) copy-start(f32[48,16,128]{2,1,0:T(8,128)} %get-tuple-element.139) | copy-start | bytes 1179652
  84.4 7.2 %collective-permute-start.7 = (f32[16,16,128]{2,1,0:T(8,128)S(1)}, f32[16,16,128]{2,1,0:T(8,128)S(1)}, u32[]{:S(2)}, u32[]{:S(2)}) collective-permute-start(f32[16,16,128]{2,1,0:T(8,128)S(1)} %slice.577), channel_id=1, source_target_pairs={{0,1},{1,2},{2,3},{3,4},{4,5},{5,6},{6,7},{7,8},{8,9},{9,10},{10,1... | collective-permute-start | bytes 393224 | tf_op jit(solution)/shard_map/ppermute | solution.py:27
  86.4 7.0 %collective-permute-start.8 = (f32[16,16,128]{2,1,0:T(8,128)S(1)}, f32[16,16,128]{2,1,0:T(8,128)S(1)}, u32[]{:S(2)}, u32[]{:S(2)}) collective-permute-start(f32[16,16,128]{2,1,0:T(8,128)S(1)} %slice.579), channel_id=1, source_target_pairs={{1,0},{2,1},{3,2},{4,3},{5,4},{6,5},{7,6},{8,7},{9,8},{10,9},{11,1... | collective-permute-start | bytes 393224 | tf_op jit(solution)/shard_map/ppermute | solution.py:28
  93.5 7.2 %collective-permute-start.10 = (f32[16,16,128]{2,1,0:T(8,128)S(1)}, f32[16,16,128]{2,1,0:T(8,128)S(1)}, u32[]{:S(2)}, u32[]{:S(2)}) collective-permute-start(f32[16,16,128]{2,1,0:T(8,128)S(1)} %slice.580), channel_id=1, source_target_pairs={{1,0},{2,1},{3,2},{4,3},{5,4},{6,5},{7,6},{8,7},{9,8},{10,9},{11,1... | collective-permute-start | bytes 393224 | tf_op jit(solution)/shard_map/ppermute | solution.py:28
  98.2 7.2 %collective-permute-start.9 = (f32[16,16,128]{2,1,0:T(8,128)S(1)}, f32[16,16,128]{2,1,0:T(8,128)S(1)}, u32[]{:S(2)}, u32[]{:S(2)}) collective-permute-start(f32[16,16,128]{2,1,0:T(8,128)S(1)} %get-tuple-element.138), channel_id=1, source_target_pairs={{0,1},{1,2},{2,3},{3,4},{4,5},{5,6},{6,7},{7,8},{8,9},{9,10},{10,1... | collective-permute-start | bytes 393224 | tf_op jit(solution)/shard_map/ppermute | solution.py:27
where the time goes:
time: 111 us; the launch traced here: 110 us
  starting transfers between devices  36.5 us (33%)
  other arithmetic  31.1 us (28%)
  waiting for transfers between devices  21.7 us (20%)
  local copies, waits for them, and re-layouts  20.2 us (18%)
    reduce_sum x4, other arithmetic, on_device(): jnp.sum(update, axis=0)  23 us
    ppermute x5, starting transfers between devices, extended_2(): after = lax.ppermute(first, axis, down)  20.2 us
    slice x9, local copies, waits for them, and re-layouts, prev_along(): rest = lax.slice_in_dim(field, 0, size - 1, axis=axis)  15.3 us
    ppermute x5, waiting for transfers between devices, extended_2(): before = lax.ppermute(last, axis, up)  14.8 us
    ppermute x5, starting transfers between devices, extended_2(): before = lax.ppermute(last, axis, up)  13.6 us
    ppermute x5, waiting for transfers between devices, extended_2(): after = lax.ppermute(first, axis, down)  6.95 us
    another operation x3, other arithmetic, on_device(): return jnp.stack(bases)  4.8 us
    ppermute x1, starting transfers between devices, shifted(): lax.ppermute(value, axis, [(source, source + steps) for source in range(f...  2.74 us
  transfers between devices with their start and end apart: 11, of which 9 were waited for; matrix products, arithmetic and copies ran while one was open for 2% of the time, Pallas kernels for 0%

commit v1 on v0

v1 whole, which is shorter than its diff:
```python
import functools

import jax
import jax.numpy as jnp
from jax import lax
from jax.experimental import pallas as pl
from jax.experimental.pallas import tpu as pltpu
from jax.sharding import PartitionSpec as P


TAIL = 8


class Lanes:
    def __init__(self, shape, width):
        lane = lax.broadcasted_iota(jnp.int32, shape, 1)
        self.width = width
        self.lanes = shape[1]
        self.rows = shape[0]
        self.lane = lane
        self.block = lane // width
        self.local = lane - self.block * width
        self.first = self.local == 0
        self.last = self.local == width - 1
        self.upper = self.local >= width // 2
        self.other = jnp.where(self.upper, self.block + 1, self.block - 1)
        self.row0 = lax.broadcasted_iota(jnp.int32, shape, 0) == 0
        self.lane0 = lane == 0

    def zm(self, v):
        return pltpu.roll(v, 1, 1)

    def zp(self, v):
        return pltpu.roll(v, self.lanes - 1, 1)

    def ym(self, v):
        return pltpu.roll(v, 1, 0)

    def yp(self, v):
        return pltpu.roll(v, self.rows - 1, 0)


class Plane:
    def __init__(self, ln, tx, txn, ty, tz, s, valid=None):
        self.ln = ln
        self.tx, self.txn = tx, txn
        self.ty = jnp.where(ln.row0, 0.0, ty)
        self.tz = jnp.where(ln.lane0, 0.0, tz)
        self.typ = ln.yp(self.ty)
        self.tzp = ln.zp(self.tz)
        e = s * (1.0 / 3.0) + ((tx + txn) + (self.ty + self.typ) + (self.tz + self.tzp))
        if valid is not None:
            e = jnp.where(valid, e, 1.0)
        self.half = 0.5 * e + s * (1.0 / 3.0)
        self.all = 1.5 * e
        self.q = 1.0 / self.all
        self.z1 = self.q * jnp.where(ln.first, self.tz, jnp.where(ln.last, self.tzp, 0.0))
        self.zm = ln.zm(self.z1)
        self.zp = ln.zp(self.z1)

    def toward(self, low):
        return self.tx if low else self.txn

    def inward(self, low):
        return self.txn if low else self.tx

    def edge(self, low):
        self.x1 = self.q * self.toward(low)
        self.o1 = 1.0 - self.z1 - self.x1

    def rim(self):
        return self.tz * self.zm + self.tzp * self.zp

    def along_y(self, v):
        return self.ty * self.ln.ym(v) + self.typ * self.ln.yp(v)


def middle(p, below, above, mz):
    ln = p.ln
    vz = p.half * p.z1 + p.tx * below.z1 + p.txn * above.z1 + p.along_y(p.z1)
    vz = vz + p.tz * jnp.where(ln.first, 1.0 - p.zm, p.zm)
    vz = vz + p.tzp * jnp.where(ln.last, 1.0 - p.zp, p.zp)
    kept = vz * mz
    return p.all - vz, kept, p.all - (vz - kept)


def second(p, edge, inner, low, mz, mx):
    below, above = (edge, inner) if low else (inner, edge)
    ln = p.ln
    first_o = ln.zm(p.z1)
    vz = p.half * p.z1 + p.tx * below.z1 + p.txn * above.z1 + p.along_y(p.z1)
    vz = vz + p.tz * jnp.where(ln.first, 1.0 - first_o, first_o)
    vz = vz + p.tzp * jnp.where(ln.last, 1.0 - p.zp, p.zp)
    vx = p.toward(low) * edge.x1
    kept_z, kept_x = vz * mz, vx * mx
    total = p.all - (vz - kept_z) - (vx - kept_x)
    return p.all - vz - vx, kept_z, kept_x, total


def edge_own(p, inner_o1, inner_z1, outer_x1, low, mz):
    ln = p.ln
    om, op = ln.zm(p.o1), ln.zp(p.o1)
    vo = p.half * p.o1 + p.toward(low) * outer_x1 + p.inward(low) * inner_o1 + p.along_y(p.o1)
    vo = vo + p.tz * jnp.where(ln.first, p.zm, om) + p.tzp * jnp.where(ln.last, p.zp, op)
    vz = p.half * p.z1 + p.inward(low) * inner_z1 + p.along_y(p.z1)
    vz = vz + p.tz * jnp.where(ln.first, om, p.zm) + p.tzp * jnp.where(ln.last, op, p.zp)
    return vo, vz * mz


def edge_total(p, mz):
    rim = p.rim()
    return p.all - (rim - rim * mz)


def edge_spill(p, own, low):
    ln = p.ln
    xm, xp = ln.zm(p.x1), ln.zp(p.x1)
    face = p.toward(low)
    vx = p.half * p.x1 + face * own.o1 + p.along_y(p.x1)
    vx = vx + p.tz * jnp.where(ln.first, 0.0, xm) + p.tzp * jnp.where(ln.last, 0.0, xp)
    vd = face * own.z1 + p.tz * jnp.where(ln.first, xm, 0.0) + p.tzp * jnp.where(ln.last, xp, 0.0)
    return vx, vd


def second_spill(p, edge, low, mz, mx):
    vx = p.toward(low) * edge.x1
    kept = vx * mx
    return kept, edge_total(p, mz) - (vx - kept)


def store(ln, dst, layer, plane, blocks, own, other, total):
    scale = 1.0 / total
    own = own * scale
    other = jnp.zeros_like(own) if other is None else other * scale
    for k in range(blocks):
        dst[layer, k, plane] = jnp.where(ln.block == k, own, jnp.where(ln.other == k, other, 0.0))


def pack_kernel(n, width, tx, ty, tz, s, reach, up, down, masks, own_masks, sems):
    copies = []

    def copy(src, dst):
        c = pltpu.make_async_copy(src, dst, sems.at[len(copies)])
        c.start()
        copies.append(c)

    copy(tx.at[pl.ds(0, 3)], down.at[pl.ds(0, 3)])
    for i, a in enumerate((ty, tz, s)):
        copy(a.at[pl.ds(0, 2)], down.at[pl.ds(3 + 2 * i, 2)])
    for i, a in enumerate((tx, ty, tz, s)):
        copy(a.at[pl.ds(n - 2, 2)], up.at[pl.ds(2 * i, 2)])
    layers, blocks, _ = reach.shape
    lanes = masks.shape[-1]
    shape = (blocks, lanes)
    k = lax.broadcasted_iota(jnp.int32, shape, 0)
    lane = lax.broadcasted_iota(jnp.int32, shape, 1)
    block = lane // width
    local = lane - block * width
    zero = jnp.zeros((1, lanes), jnp.float32)

    def row(cond):
        return jnp.sum(jnp.where(cond, 1.0, 0.0), axis=0, keepdims=True)

    for layer in range(layers):
        r = [jnp.broadcast_to(reach[layer, :, j : j + 1], shape) for j in range(4)]
        from_below = (block - 1 == k) & (local < width // 2) & (r[3] >= local + 1)
        from_above = (block + 1 == k) & (local >= width // 2) & (r[2] >= width - local)
        rows = [
            row(from_below | from_above),
            row((block == k) & (r[0] >= 2)),
            row((block == k) & (r[1] >= 2)),
        ]
        own_masks[layer] = jnp.concatenate(rows + [zero] * (TAIL - len(rows)), axis=0)
    copy(own_masks, masks)
    copy(own_masks.at[0], down.at[9, pl.ds(0, TAIL)])
    copy(own_masks.at[layers - 1], up.at[8, pl.ds(0, TAIL)])
    for c in copies:
        c.wait()


def bulk_kernel(width, blocks, tx, ty, tz, s, masks, out, zeros, buf, faces, sems):
    layers = masks.shape[0]
    n, rows, lanes = faces.shape[1:]
    fetch = [pltpu.make_async_copy(a, faces.at[i], sems.at[i]) for i, a in enumerate((tx, ty, tz, s))]
    for c in fetch:
        c.start()
    zeros[...] = jnp.zeros(zeros.shape, jnp.float32)
    depth = zeros.shape[0]
    clears = []
    for layer in range(layers):
        for k in range(blocks):
            for start in (0, 3 * width - depth):
                sem = sems.at[4 + len(clears)]
                c = pltpu.make_async_copy(zeros, out.at[layer, k, pl.ds(start, depth)], sem)
                c.start()
                clears.append(c)
    ln = Lanes((rows, lanes), width)
    for c in fetch:
        c.wait()

    def plane(p):
        return Plane(ln, faces[0, p], faces[0, p + 1], faces[1, p], faces[2, p], faces[3, p])

    sends = []
    for layer in range(layers):
        base = layer * width
        mz = masks[layer, 0:1]
        low, high = layer == 0, layer == layers - 1
        origin = base - width
        if not low:
            ma = masks[layer - 1, 0:1]
            to_above, to_below = masks[layer - 1, 2:3], masks[layer, 1:2]
            a3, a2, a1 = (plane(base - i) for i in (3, 2, 1))
            b0, b1, b2 = (plane(base + i) for i in (0, 1, 2))
            a1.edge(False)
            b0.edge(True)
            prev = origin - width
            put = functools.partial(store, ln, buf)
            vo, vz, vx, total = second(a2, a1, a3, False, ma, to_below)
            put(layer - 1, base - 2 - prev - (width - 2), blocks, vo, vz, total)
            put(layer, base - 2 - origin - (width - 2), blocks, vx, None, total)
            vo, vz = edge_own(a1, 1.0 - a2.z1, a2.z1, b0.x1, False, ma)
            vx, vd = edge_spill(a1, b0, False)
            total = edge_total(a1, ma)
            put(layer - 1, base - 1 - prev - (width - 2), blocks, vo, vz, total)
            put(layer, base - 1 - origin - (width - 2), blocks, vx, vd, total)
            vo, vz = edge_own(b0, 1.0 - b1.z1, b1.z1, a1.x1, True, mz)
            vx, vd = edge_spill(b0, a1, True)
            total = edge_total(b0, mz)
            put(layer, base - origin - (width - 2), blocks, vo, vz, total)
            put(layer - 1, base - prev - (width - 2), blocks, vx, vd, total)
            vo, vz, vx, total = second(b1, b0, b2, True, mz, to_above)
            put(layer, base + 1 - origin - (width - 2), blocks, vo, vz, total)
            put(layer - 1, base + 1 - prev - (width - 2), blocks, vx, None, total)
            sends.append(send_layer(layer - 1, layers, width, blocks, buf, out, sems))
        planes = [plane(base + a) for a in range(1, width - 1)]
        for a in range(2, width - 2):
            vo, vz, total = middle(planes[a - 1], planes[a - 2], planes[a], mz)
            store(ln, buf, layer, a + 2, blocks, vo, vz, total)
        if high:
            sends.append(send_layer(layer, layers, width, blocks, buf, out, sems))
    for group in sends:
        for c in group:
            c.wait()
    for c in clears:
        c.wait()


def span(layer, layers, width):
    return (4 if layer == 0 else 0), (width if layer == layers - 1 else width + 4)


def send_layer(layer, layers, width, blocks, buf, out, sems):
    low, high = span(layer, layers, width)
    group = []
    for k in range(blocks):
        c = pltpu.make_async_copy(
            buf.at[layer, k, pl.ds(low, high - low)],
            out.at[layer, k, pl.ds(width - 2 + low, high - low)],
            sems.at[4 + 2 * layers * blocks + layer * blocks + k],
        )
        c.start()
        group.append(c)
    return group


def edge_kernel(
    n, width, blocks, axis, count, tx, ty, tz, s, masks, below, above, held, out,
    lo, hi, lob, hib, buf, sems,
):
    del held
    layers = masks.shape[0]
    copies = []

    def copy(src, dst):
        c = pltpu.make_async_copy(src, dst, sems.at[len(copies)])
        c.start()
        copies.append(c)

    copy(below, lob)
    copy(above, hib)
    for i, a in enumerate((tx, ty, tz, s)):
        copy(a.at[pl.ds(0, 4)], lo.at[i])
        copy(a.at[pl.ds(n - 4, 4)], hi.at[i])
    me = lax.axis_index(axis)
    for c in copies:
        c.wait()
    rows, lanes = lo.shape[2:]
    ln = Lanes((rows, lanes), width)
    put = functools.partial(store, ln, buf)
    low_ok, high_ok = me > 0, me < count - 1

    tx0 = jnp.where(low_ok, lo[0, 0], 0.0)
    a2 = Plane(ln, lob[0], lob[1], lob[2], lob[4], lob[6], low_ok)
    a1 = Plane(ln, lob[1], tx0, lob[3], lob[5], lob[7], low_ok)
    ma, to_above = lob[8, 0:1], lob[8, 2:3]
    mz, to_below = masks[0, 0:1], masks[0, 1:2]
    b0 = Plane(ln, tx0, lo[0, 1], lo[1, 0], lo[2, 0], lo[3, 0])
    b1, b2 = (Plane(ln, lo[0, i], lo[0, i + 1], lo[1, i], lo[2, i], lo[3, i]) for i in (1, 2))
    a1.edge(False)
    b0.edge(True)
    vx, total = second_spill(a2, a1, False, ma, to_below)
    put(0, 0, blocks, vx, None, total)
    vx, vd = edge_spill(a1, b0, False)
    put(0, 1, blocks, vx, vd, edge_total(a1, ma))
    vo, vz = edge_own(b0, 1.0 - b1.z1, b1.z1, a1.x1, True, mz)
    put(0, 2, blocks, vo, vz, edge_total(b0, mz))
    vo, vz, _, total = second(b1, b0, b2, True, mz, to_above)
    put(0, 3, blocks, vo, vz, total)
    sends = []

    def send(side, layer, start):
        for k in range(blocks):
            c = pltpu.make_async_copy(
                buf.at[side, k], out.at[layer, k, pl.ds(start, 4)], sems.at[len(copies) + len(sends)]
            )
            c.start()
            sends.append(c)

    send(0, 0, width - 2)

    mz, to_above = masks[layers - 1, 0:1], masks[layers - 1, 2:3]
    mb, to_below = hib[9, 0:1], hib[9, 1:2]
    a3, a2 = (Plane(ln, hi[0, i], hi[0, i + 1], hi[1, i], hi[2, i], hi[3, i]) for i in (1, 2))
    a1 = Plane(ln, hi[0, 3], hib[0], hi[1, 3], hi[2, 3], hi[3, 3])
    b0 = Plane(ln, hib[0], hib[1], hib[3], hib[5], hib[7], high_ok)
    b1 = Plane(ln, hib[1], hib[2], hib[4], hib[6], hib[8], high_ok)
    a1.edge(False)
    b0.edge(True)
    vo, vz, _, total = second(a2, a1, a3, False, mz, to_below)
    put(1, 0, blocks, vo, vz, total)
    vo, vz = edge_own(a1, 1.0 - a2.z1, a2.z1, b0.x1, False, mz)
    put(1, 1, blocks, vo, vz, edge_total(a1, mz))
    vx, vd = edge_spill(b0, a1, True)
    put(1, 2, blocks, vx, vd, edge_total(b0, mb))
    vx, total = second_spill(b1, b0, True, mb, to_above)
    put(1, 3, blocks, vx, None, total)
    send(1, layers - 1, 2 * width - 2)
    for c in sends:
        c.wait()


def on_device(trans_east, trans_north, trans_up, storage, support_reach, *, axis, count):
    layers, blocks, _ = support_reach.shape
    n, rows, lanes = trans_east.shape
    width = n // layers
    f32 = jnp.float32
    anywhere = pl.BlockSpec(memory_space=pl.ANY)
    vmem = pl.BlockSpec(memory_space=pltpu.VMEM)
    params = pltpu.CompilerParams(vmem_limit_bytes=16 * 2**20)
    faces = (trans_east, trans_north, trans_up, storage)

    up, down, masks = pl.pallas_call(
        functools.partial(pack_kernel, n, width),
        out_shape=(
            jax.ShapeDtypeStruct((9, rows, lanes), f32),
            jax.ShapeDtypeStruct((10, rows, lanes), f32),
            jax.ShapeDtypeStruct((layers, TAIL, lanes), f32),
        ),
        in_specs=[anywhere] * 4 + [vmem],
        out_specs=(anywhere,) * 3,
        scratch_shapes=[pltpu.VMEM((layers, TAIL, lanes), f32), pltpu.SemaphoreType.DMA((11,))],
        compiler_params=params,
        name="pack",
    )(*faces, support_reach)
    below = lax.ppermute(up, axis, [(i, i + 1) for i in range(count - 1)])
    above = lax.ppermute(down, axis, [(i + 1, i) for i in range(count - 1)])

    out_shape = jax.ShapeDtypeStruct((layers, blocks, 3 * width, rows, lanes), f32)
    bulk = pl.pallas_call(
        functools.partial(bulk_kernel, width, blocks),
        out_shape=out_shape,
        in_specs=[anywhere] * 4 + [vmem],
        out_specs=anywhere,
        scratch_shapes=[
            pltpu.VMEM((width - 2, rows, lanes), f32),
            pltpu.VMEM((layers, blocks, width + 4, rows, lanes), f32),
            pltpu.VMEM((4, n, rows, lanes), f32),
            pltpu.SemaphoreType.DMA((4 + 3 * layers * blocks,)),
        ],
        compiler_params=params,
        cost_estimate=pl.CostEstimate(flops=10**7, bytes_accessed=7 * 10**6, transcendentals=0),
        name="bulk",
    )(*faces, masks)
    return pl.pallas_call(
        functools.partial(edge_kernel, n, width, blocks, axis, count),
        out_shape=out_shape,
        in_specs=[anywhere] * 4 + [vmem] + [anywhere] * 3,
        out_specs=anywhere,
        scratch_shapes=[
            pltpu.VMEM((4, 4, rows, lanes), f32),
            pltpu.VMEM((4, 4, rows, lanes), f32),
            pltpu.VMEM((9, rows, lanes), f32),
            pltpu.VMEM((10, rows, lanes), f32),
            pltpu.VMEM((2, blocks, 4, rows, lanes), f32),
            pltpu.SemaphoreType.DMA((10 + 2 * blocks,)),
        ],
        input_output_aliases={7: 0},
        compiler_params=params,
        cost_estimate=pl.CostEstimate(flops=10**6, bytes_accessed=10**6, transcendentals=0),
        name="edges",
    )(*faces, masks, below, above, bulk)


def solution(mesh):
    spread = P(("groups", "blk"))
    return jax.shard_map(
        functools.partial(on_device, axis="blk", count=mesh.shape["blk"]),
        mesh=mesh,
        in_specs=(spread,) * 5,
        out_specs=spread,
        check_vma=False,
    )
```

time: 111 us -> 16.6 us (0.15)
  the two profiles are of different devices: /device:TPU:8 before, /device:TPU:1 now
where the time goes in v1:
time: 16.6 us; the launch traced here: 16.3 us
  starting transfers between devices  6.46 us (39%)
  Pallas kernels  5.21 us (31%)
  local copies, waits for them, and re-layouts  4.56 us (27%)
    unnamed x9, local copies, waits for them, and re-layouts  4.56 us
    ppermute x1, starting transfers between devices, on_device(): below = lax.ppermute(up, axis, [(i, i + 1) for i in range(count - 1)])  4.49 us
    pallas_call x1, Pallas kernels, on_device(): pl.pallas_call(functools.partial(bulk_kernel, width, blocks), out_shape=o...  3.05 us
    ppermute x1, starting transfers between devices, on_device(): above = lax.ppermute(down, axis, [(i + 1, i) for i in range(count - 1)])  1.97 us
    pallas_call x1, Pallas kernels, on_device(): pl.pallas_call(functools.partial(edge_kernel, n, width, blocks, axis, cou...  1.79 us
    pallas_call x1, Pallas kernels, on_device(): pl.pallas_call(functools.partial(pack_kernel, n, width), out_shape=(jax.S...  0.37 us
  transfers between devices with their start and end apart: 2, of which 0 were waited for; matrix products, arithmetic and copies ran while one was open for 0% of the time, Pallas kernels for 19%

profile of v1, /device:TPU:1, one launch (start us, length us, event | category | flops | bytes accessed | tf_op | source)
XLA Modules:
  0.0 16.3 jit_solution(3245131788349237604)
XLA Ops:
  0.0 0.8 %copy.7.reach = s32[2,8,4]{2,1,0:T(8,128)S(1)} copy(s32[2,8,4]{1,2,0:T(4,128)} %param.9) | data formatting | bytes 512 | tf_op args[4]
  0.8 0.0 copy-start
  0.8 0.9 %copy-done = f32[32,16,128]{2,1,0:T(8,128)S(1)} copy-done((f32[32,16,128]{2,1,0:T(8,128)S(1)}, f32[32,16,128]{2,1,0:T(8,128)}, u32[]{:S(2)}) %copy-start) | copy-done | bytes 262168
  1.7 0.0 copy-start.1
  1.7 0.9 %copy-done.1 = f32[32,16,128]{2,1,0:T(8,128)S(1)} copy-done((f32[32,16,128]{2,1,0:T(8,128)S(1)}, f32[32,16,128]{2,1,0:T(8,128)}, u32[]{:S(2)}) %copy-start.1) | copy-done | bytes 262168
  2.7 0.0 copy-start.2
  2.7 0.9 %copy-done.2 = f32[32,16,128]{2,1,0:T(8,128)S(1)} copy-done((f32[32,16,128]{2,1,0:T(8,128)S(1)}, f32[32,16,128]{2,1,0:T(8,128)}, u32[]{:S(2)}) %copy-start.2) | copy-done | bytes 262168
  3.6 0.0 copy-start.3
  3.6 0.9 %copy-done.3 = f32[32,16,128]{2,1,0:T(8,128)S(1)} copy-done((f32[32,16,128]{2,1,0:T(8,128)S(1)}, f32[32,16,128]{2,1,0:T(8,128)}, u32[]{:S(2)}) %copy-start.3) | copy-done | bytes 262168
  4.6 0.4 %pack.1 = (f32[9,16,128]{2,1,0:T(8,128)S(1)}, f32[10,16,128]{2,1,0:T(8,128)S(1)}, f32[2,8,128]{2,1,0:T(8,128)S(1)}) custom-call(f32[32,16,128]{2,1,0:T(8,128)S(1)} %copy-done, f32[32,16,128]{2,1,0:T(8,128)S(1)} %copy-done.1, f32[32,16,128]{2,1,0:T(8,128)S(1)} %copy-done.2, f32[32,16,128]{2,1,0:T(8,128)S(1)} %copy-done.3, s32[2,8,4]{2,1,0:T(8,128)S(1)} %copy.7.reach), custom_call_target="tpu_custom_call" | custom-call | tf_op jit(solution)/shard_map/pack/pallas_call | solution.py:353
  5.0 2.0 %collective-permute-start.1 = (f32[10,16,128]{2,1,0:T(8,128)S(1)}, f32[10,16,128]{2,1,0:T(8,128)S(1)}, u32[]{:S(2)}, u32[]{:S(2)}) collective-permute-start(f32[10,16,128]{2,1,0:T(8,128)S(1)} %get-tuple-element.10), channel_id=1, source_target_pairs={{1,0},{2,1},{3,2},{4,3},{5,4},{6,5},{7,6},{8,7},{9,8},{10,9},{11,1... | collective-permute-start | bytes 245768 | tf_op jit(solution)/shard_map/ppermute | solution.py:367
  6.9 4.5 %collective-permute-start = (f32[9,16,128]{2,1,0:T(8,128)S(1)}, f32[9,16,128]{2,1,0:T(8,128)S(1)}, u32[]{:S(2)}, u32[]{:S(2)}) collective-permute-start(f32[9,16,128]{2,1,0:T(8,128)S(1)} %get-tuple-element.9), channel_id=1, source_target_pairs={{0,1},{1,2},{2,3},{3,4},{4,5},{5,6},{6,7},{7,8},{8,9},{9,10},{10,1... | collective-permute-start | bytes 221192 | tf_op jit(solution)/shard_map/ppermute | solution.py:366
  11.4 3.0 %bulk.1.held = f32[2,8,48,16,128]{4,3,2,1,0:T(8,128)} custom-call(f32[32,16,128]{2,1,0:T(8,128)S(1)} %copy-done, f32[32,16,128]{2,1,0:T(8,128)S(1)} %copy-done.1, f32[32,16,128]{2,1,0:T(8,128)S(1)} %copy-done.2, f32[32,16,128]{2,1,0:T(8,128)S(1)} %copy-done.3, f32[2,8,128]{2,1,0:T(8,128)S(1)} %get-tuple-element.8.masks), custom_call_target="tpu_custom_call" | custom-call | flops 10000000 | bytes 7000000 | tf_op jit(solution)/shard_map/bulk/pallas_call | solution.py:370
  14.5 0.0 collective-permute-done.below
  14.5 0.0 collective-permute-done.1.above
  14.5 1.8 %edges.1 = f32[2,8,48,16,128]{4,3,2,1,0:T(8,128)} custom-call(f32[32,16,128]{2,1,0:T(8,128)S(1)} %copy-done, f32[32,16,128]{2,1,0:T(8,128)S(1)} %copy-done.1, f32[32,16,128]{2,1,0:T(8,128)S(1)} %copy-done.2, f32[32,16,128]{2,1,0:T(8,128)S(1)} %copy-done.3, f32[2,8,128]{2,1,0:T(8,128)S(1)} %get-tuple-element.8.masks, ...), custom_call_target="tpu_custom_call", output_to_operand_aliasing={{}: (7, {})} | custom-call | flops 1000000 | bytes 1000000 | tf_op jit(solution)/shard_map/edges/pallas_call | solution.py:385
Async XLA Ops:
  0.8 0.9 %copy-start = (f32[32,16,128]{2,1,0:T(8,128)S(1)}, f32[32,16,128]{2,1,0:T(8,128)}, u32[]{:S(2)}) copy-start(f32[32,16,128]{2,1,0:T(8,128)} %tx.5) | copy-start | bytes 786436
  1.7 0.9 %copy-start.1 = (f32[32,16,128]{2,1,0:T(8,128)S(1)}, f32[32,16,128]{2,1,0:T(8,128)}, u32[]{:S(2)}) copy-start(f32[32,16,128]{2,1,0:T(8,128)} %ty.5) | copy-start | bytes 786436
  2.7 0.9 %copy-start.2 = (f32[32,16,128]{2,1,0:T(8,128)S(1)}, f32[32,16,128]{2,1,0:T(8,128)}, u32[]{:S(2)}) copy-start(f32[32,16,128]{2,1,0:T(8,128)} %tz.5) | copy-start | bytes 786436
  3.6 0.9 %copy-start.3 = (f32[32,16,128]{2,1,0:T(8,128)S(1)}, f32[32,16,128]{2,1,0:T(8,128)}, u32[]{:S(2)}) copy-start(f32[32,16,128]{2,1,0:T(8,128)} %s.5) | copy-start | bytes 786436
  5.0 9.5 %collective-permute-start.1 = (f32[10,16,128]{2,1,0:T(8,128)S(1)}, f32[10,16,128]{2,1,0:T(8,128)S(1)}, u32[]{:S(2)}, u32[]{:S(2)}) collective-permute-start(f32[10,16,128]{2,1,0:T(8,128)S(1)} %get-tuple-element.10), channel_id=1, source_target_pairs={{1,0},{2,1},{3,2},{4,3},{5,4},{6,5},{7,6},{8,7},{9,8},{10,9},{11,1... | collective-permute-start | bytes 245768 | tf_op jit(solution)/shard_map/ppermute | solution.py:367
  6.9 7.6 %collective-permute-start = (f32[9,16,128]{2,1,0:T(8,128)S(1)}, f32[9,16,128]{2,1,0:T(8,128)S(1)}, u32[]{:S(2)}, u32[]{:S(2)}) collective-permute-start(f32[9,16,128]{2,1,0:T(8,128)S(1)} %get-tuple-element.9), channel_id=1, source_target_pairs={{0,1},{1,2},{2,3},{3,4},{4,5},{5,6},{6,7},{7,8},{8,9},{9,10},{10,1... | collective-permute-start | bytes 221192 | tf_op jit(solution)/shard_map/ppermute | solution.py:366
